TPU v7x, 512 devices: a whole 4x8x8 slice. The times are simulated.
512 devices in a mesh: dp: 8 (over z), ctx: 64 (over y, x, core).
Axes of the slice: x: 4, y: 8, z: 8, core: 2. Of those that a mesh axis runs over, the one named last changes fastest.
Arguments:
- query_act: bfloat16 [8, 8192, 2048], P('dp', 'ctx'), may hold values from -6 to 6
- key_act: bfloat16 [8, 8192, 2048], P('dp', 'ctx'), may hold values from -6 to 6
- value_act: bfloat16 [8, 8192, 2048], P('dp', 'ctx'), may hold values from -6 to 6
- grad_out: bfloat16 [8, 8192, 2048], P('dp', 'ctx'), may hold values from -16 to 16
- filter_taps: bfloat16 [128, 2048], replicated, may hold values from -2.5 to 2.5
Outputs:
- output_act: bfloat16 [8, 8192, 2048], P('dp', 'ctx')
- grad_query: bfloat16 [8, 8192, 2048], P('dp', 'ctx')
- grad_key: bfloat16 [8, 8192, 2048], P('dp', 'ctx')
- grad_value: bfloat16 [8, 8192, 2048], P('dp', 'ctx')
- grad_filter: float32 [128, 2048], P(None, 'ctx')
All inputs are finite; a program needn't handle non-finite values.
Results may differ from a plain program's by a relative error of at most 0.0065.
Values may be sent and summed in bfloat16 or wider, within the bound.
A program may use at most 64 MiB of HBM per device.

v0:
```python
import math

import jax
import jax.numpy as jnp
from jax import lax
from jax.sharding import PartitionSpec as P

tap_block = 16


def from_behind(array, axis, by):
    devices = lax.axis_size(axis)
    pairs = [(i, i + by) for i in range(devices) if 0 <= i + by < devices]
    return lax.ppermute(array, axis, pairs)


def forward_taps(padded, weights, length):
    tap_count = weights.shape[0]

    def forward_advance(number, running):
        first = number * tap_block
        window = lax.dynamic_slice_in_dim(
            padded, tap_count - tap_block - first, length + tap_block - 1, 0
        )
        coeffs = lax.dynamic_slice_in_dim(weights, first, tap_block, 0)
        for inner in range(tap_block):
            start_row = tap_block - 1 - inner
            running = running + coeffs[inner] * window[start_row : start_row + length]
        return running

    initial = jnp.zeros((length, padded.shape[1]), jnp.float32)
    return lax.fori_loop(0, tap_count // tap_block, forward_advance, initial)


def backward_taps(extended, weights, length):
    tap_count = weights.shape[0]

    def backward_advance(number, running):
        first = number * tap_block
        window = lax.dynamic_slice_in_dim(extended, first, length + tap_block - 1, 0)
        coeffs = lax.dynamic_slice_in_dim(weights, first, tap_block, 0)
        for inner in range(tap_block):
            running = running + coeffs[inner] * window[inner : inner + length]
        return running

    initial = jnp.zeros((length, extended.shape[1]), jnp.float32)
    return lax.fori_loop(0, tap_count // tap_block, backward_advance, initial)


def lag_sums(grad_float, padded, tap_count):
    length = grad_float.shape[0]

    def lag_advance(number, running):
        first = number * tap_block
        window = lax.dynamic_slice_in_dim(
            padded, tap_count - tap_block - first, length + tap_block - 1, 0
        )
        lines = []
        for inner in range(tap_block):
            start_row = tap_block - 1 - inner
            lines.append(jnp.sum(grad_float * window[start_row : start_row + length], axis=0))
        return lax.dynamic_update_slice_in_dim(running, jnp.stack(lines), first, 0)

    initial = jnp.zeros((tap_count, padded.shape[1]), jnp.float32)
    return lax.fori_loop(0, tap_count // tap_block, lag_advance, initial)


def per_device(query_act, key_act, value_act, grad_out, filter_taps):
    query_rows = query_act[0].astype(jnp.float32)
    key_rows = key_act[0].astype(jnp.float32)
    value_rows = value_act[0].astype(jnp.float32)
    grad_rows = grad_out[0].astype(jnp.float32)
    length = query_rows.shape[0]
    channels = query_rows.shape[1]
    tap_count = filter_taps.shape[0]
    weights = filter_taps.astype(jnp.float32)
    kv_product = (key_rows * value_rows).astype(jnp.bfloat16)
    gate_grad = (grad_rows * query_rows).astype(jnp.bfloat16)
    before = from_behind(kv_product[length - tap_count + 1 :], "ctx", 1)
    beyond = from_behind(gate_grad[: tap_count - 1], "ctx", -1)
    padded = jnp.concatenate([before, kv_product], axis=0)
    filtered = forward_taps(padded, weights, length)
    output_rows = (query_rows * filtered).astype(jnp.bfloat16)
    grad_query_rows = (grad_rows * filtered).astype(jnp.bfloat16)
    extended = jnp.concatenate([gate_grad, beyond], axis=0)
    flowing = backward_taps(extended, weights, length)
    grad_key_rows = (flowing * value_rows).astype(jnp.bfloat16)
    grad_value_rows = (flowing * key_rows).astype(jnp.bfloat16)
    token_count = length * lax.axis_size("ctx") * lax.axis_size("dp")
    partial_sum = lag_sums(gate_grad.astype(jnp.float32), padded, tap_count) * (
        1.0 / math.sqrt(token_count)
    )
    share_width = channels // lax.axis_size("ctx")
    summed = lax.psum(partial_sum, ("dp", "ctx"))
    own_filter = lax.dynamic_slice_in_dim(
        summed, lax.axis_index("ctx") * share_width, share_width, 1
    )
    return (
        output_rows[None],
        grad_query_rows[None],
        grad_key_rows[None],
        grad_value_rows[None],
        own_filter,
    )


def solution(mesh):
    in_specs = (
        P("dp", "ctx", None),
        P("dp", "ctx", None),
        P("dp", "ctx", None),
        P("dp", "ctx", None),
        P(),
    )
    out_specs = (
        P("dp", "ctx", None),
        P("dp", "ctx", None),
        P("dp", "ctx", None),
        P("dp", "ctx", None),
        P(None, "ctx"),
    )
    return jax.shard_map(
        per_device, mesh=mesh, in_specs=in_specs, out_specs=out_specs, check_vma=False
    )
```

profile of v0, /device:TPU:1, one launch (start us, length us, event | category | flops | bytes accessed | tf_op | source)
XLA Modules:
  0.0 410.5 jit_solution(5974135181188779003)
XLA Ops:
  8.6 8.8 %collective-permute-start.1 = (bf16[127,2048]{1,0:T(8,128)(2,1)S(1)}, bf16[127,2048]{1,0:T(8,128)(2,1)}, u32[]{:S(2)}, u32[]{:S(2)}) collective-permute-start(bf16[127,2048]{1,0:T(8,128)(2,1)S(1)} %bitcast.171), channel_id=1, source_target_pairs={{1,0},{2,1},{3,2},{4,3},{5,4},{6,5},{7,6},{8,7},{9,8},{10,9},{11,1... | collective-permute-start | bytes 1560584 | tf_op jit(solution)/shard_map/ppermute | solution.py:14
  21.4 42.1 %while.47 = (s32[]{:T(128)}, f32[128,2048]{1,0:T(8,128)S(1)}, f32[128,2048]{1,0:T(8,128)}, bf16[255,2048]{1,0:T(8,128)(2,1)S(1)}, s32[]{:T(128)}, /*index=5*/s32...) while((s32[]{:T(128)}, f32[128,2048]{1,0:T(8,128)S(1)}, ...), condition=%wide.region_3.0_spmd.clone, body=%wide.region_2.0_spmd.clone.sunk | while | flops 12845095 | bytes 10879758 | solution.py:47
  21.5 1.7 constant_dynamic-slice_fusion.36
  23.1 3.4 fusion.45
  26.6 1.9 constant_dynamic-slice_fusion.36
  28.5 3.4 fusion.45
  31.9 1.7 constant_dynamic-slice_fusion.36
  33.6 3.4 fusion.45
  37.0 1.9 constant_dynamic-slice_fusion.36
  39.0 3.4 fusion.45
  42.4 1.7 constant_dynamic-slice_fusion.36
  44.2 3.4 fusion.45
  47.6 1.9 constant_dynamic-slice_fusion.36
  49.6 3.4 fusion.45
  53.0 1.7 constant_dynamic-slice_fusion.36
  54.7 3.4 fusion.45
  58.1 2.0 constant_dynamic-slice_fusion.36
  60.1 3.4 fusion.45
  63.5 2.5 fusion.36
  66.2 1.9 collective-permute-start
  68.1 6.1 %collective-permute-done = bf16[127,2048]{1,0:T(8,128)(2,1)} collective-permute-done((bf16[127,2048]{1,0:T(8,128)(2,1)S(1)}, bf16[127,2048]{1,0:T(8,128)(2,1)}, u32[]{:S(2)}, u32[]{:S(2)}) %collective-permute-start) | collective-permute-done | bytes 520224 | tf_op jit(solution)/shard_map/ppermute | solution.py:14
  76.7 41.9 %while.45 = (s32[]{:T(128)}, f32[128,2048]{1,0:T(8,128)}, bf16[255,2048]{1,0:T(8,128)(2,1)S(1)}, f32[128,2048]{1,0:T(8,128)S(1)}, s32[]{:T(128)}, /*index=5*/s32...) while((s32[]{:T(128)}, f32[128,2048]{1,0:T(8,128)}, ...), condition=%wide.region_21.0_spmd, body=%wide.region_4.0_spmd.sunk | while | flops 12550169 | bytes 10093105 | solution.py:65
  76.7 4.3 %multiply_reduce_fusion.17 = (f32[2048]{0:T(1024)S(1)}, f32[2048]{0:T(1024)S(1)}, f32[2048]{0:T(1024)S(1)}, f32[2048]{0:T(1024)S(1)}, f32[2048]{0:T(1024)S(1)}, ...) fusion(f32[128,2048]{1,0:T(8,128)S(1)} %get-tuple-element.787, ...), kind=kLoop, calls=%fused_computation.clone.1 | loop fusion | flops 12550144 | bytes 9568320 | tf_op jit(solution)/shard_map/while/body/eval_jaxpr/reduce_sum | solution.py:61
  81.9 4.3 %multiply_reduce_fusion.17 = (f32[2048]{0:T(1024)S(1)}, f32[2048]{0:T(1024)S(1)}, f32[2048]{0:T(1024)S(1)}, f32[2048]{0:T(1024)S(1)}, f32[2048]{0:T(1024)S(1)}, ...) fusion(f32[128,2048]{1,0:T(8,128)S(1)} %get-tuple-element.787, ...), kind=kLoop, calls=%fused_computation.clone.1 | loop fusion | flops 12550144 | bytes 9568320 | tf_op jit(solution)/shard_map/while/body/eval_jaxpr/reduce_sum | solution.py:61
  87.2 4.3 %multiply_reduce_fusion.17 = (f32[2048]{0:T(1024)S(1)}, f32[2048]{0:T(1024)S(1)}, f32[2048]{0:T(1024)S(1)}, f32[2048]{0:T(1024)S(1)}, f32[2048]{0:T(1024)S(1)}, ...) fusion(f32[128,2048]{1,0:T(8,128)S(1)} %get-tuple-element.787, ...), kind=kLoop, calls=%fused_computation.clone.1 | loop fusion | flops 12550144 | bytes 9568320 | tf_op jit(solution)/shard_map/while/body/eval_jaxpr/reduce_sum | solution.py:61
  92.4 4.3 %multiply_reduce_fusion.17 = (f32[2048]{0:T(1024)S(1)}, f32[2048]{0:T(1024)S(1)}, f32[2048]{0:T(1024)S(1)}, f32[2048]{0:T(1024)S(1)}, f32[2048]{0:T(1024)S(1)}, ...) fusion(f32[128,2048]{1,0:T(8,128)S(1)} %get-tuple-element.787, ...), kind=kLoop, calls=%fused_computation.clone.1 | loop fusion | flops 12550144 | bytes 9568320 | tf_op jit(solution)/shard_map/while/body/eval_jaxpr/reduce_sum | solution.py:61
  97.7 4.3 %multiply_reduce_fusion.17 = (f32[2048]{0:T(1024)S(1)}, f32[2048]{0:T(1024)S(1)}, f32[2048]{0:T(1024)S(1)}, f32[2048]{0:T(1024)S(1)}, f32[2048]{0:T(1024)S(1)}, ...) fusion(f32[128,2048]{1,0:T(8,128)S(1)} %get-tuple-element.787, ...), kind=kLoop, calls=%fused_computation.clone.1 | loop fusion | flops 12550144 | bytes 9568320 | tf_op jit(solution)/shard_map/while/body/eval_jaxpr/reduce_sum | solution.py:61
  102.9 4.3 %multiply_reduce_fusion.17 = (f32[2048]{0:T(1024)S(1)}, f32[2048]{0:T(1024)S(1)}, f32[2048]{0:T(1024)S(1)}, f32[2048]{0:T(1024)S(1)}, f32[2048]{0:T(1024)S(1)}, ...) fusion(f32[128,2048]{1,0:T(8,128)S(1)} %get-tuple-element.787, ...), kind=kLoop, calls=%fused_computation.clone.1 | loop fusion | flops 12550144 | bytes 9568320 | tf_op jit(solution)/shard_map/while/body/eval_jaxpr/reduce_sum | solution.py:61
  108.1 4.3 %multiply_reduce_fusion.17 = (f32[2048]{0:T(1024)S(1)}, f32[2048]{0:T(1024)S(1)}, f32[2048]{0:T(1024)S(1)}, f32[2048]{0:T(1024)S(1)}, f32[2048]{0:T(1024)S(1)}, ...) fusion(f32[128,2048]{1,0:T(8,128)S(1)} %get-tuple-element.787, ...), kind=kLoop, calls=%fused_computation.clone.1 | loop fusion | flops 12550144 | bytes 9568320 | tf_op jit(solution)/shard_map/while/body/eval_jaxpr/reduce_sum | solution.py:61
  113.3 4.3 %multiply_reduce_fusion.17 = (f32[2048]{0:T(1024)S(1)}, f32[2048]{0:T(1024)S(1)}, f32[2048]{0:T(1024)S(1)}, f32[2048]{0:T(1024)S(1)}, f32[2048]{0:T(1024)S(1)}, ...) fusion(f32[128,2048]{1,0:T(8,128)S(1)} %get-tuple-element.787, ...), kind=kLoop, calls=%fused_computation.clone.1 | loop fusion | flops 12550144 | bytes 9568320 | tf_op jit(solution)/shard_map/while/body/eval_jaxpr/reduce_sum | solution.py:61
  121.2 42.6 %while.46 = (s32[]{:T(128)}, f32[128,2048]{1,0:T(8,128)S(1)}, f32[128,2048]{1,0:T(8,128)}, bf16[255,2048]{1,0:T(8,128)(2,1)S(1)}, s32[]{:T(128)}, /*index=5*/s32...) while((s32[]{:T(128)}, f32[128,2048]{1,0:T(8,128)S(1)}, ...), condition=%wide.region_1.0_spmd.clone, body=%wide.region_0.0_spmd.clone.sunk | while | flops 12845097 | bytes 10879787 | solution.py:32
  121.3 1.7 constant_dynamic-slice_fusion.35
  123.0 3.5 fusion.44
  126.4 1.9 constant_dynamic-slice_fusion.35
  128.4 3.5 fusion.44
  131.9 1.7 constant_dynamic-slice_fusion.35
  133.6 3.5 fusion.44
  137.0 1.9 constant_dynamic-slice_fusion.35
  139.0 3.5 fusion.44
  142.5 1.7 constant_dynamic-slice_fusion.35
  144.2 3.5 fusion.44
  147.7 1.9 constant_dynamic-slice_fusion.35
  149.7 3.5 fusion.44
  153.2 1.7 constant_dynamic-slice_fusion.35
  154.9 3.5 fusion.44
  158.4 2.0 constant_dynamic-slice_fusion.35
  160.4 3.5 fusion.44
  165.1 237.3 %all-reduce.2.cloned.1.call-done = f32[128,2048]{0,1:T(8,128)} async-done(((f32[128,2048]{0,1:T(8,128)}), f32[128,2048]{0,1:T(8,128)}) %all-reduce.2.cloned.1.call-update) | async-done | bytes 1048592 | tf_op jit(solution)/shard_map/psum | solution.py:94
  (41 shorter events, 20.3 us)
Async XLA Ops:
  7.2 10.3 %copy-start.4 = (bf16[128,2048]{1,0:T(8,128)(2,1)S(1)}, bf16[128,2048]{1,0:T(8,128)(2,1)}, u32[]{:S(2)}) copy-start(bf16[128,2048]{1,0:T(8,128)(2,1)} %param.15) | copy-start | bytes 1572868
  7.2 395.2 %all-reduce.2.cloned.1.call-start = ((), (), s32[]{:S(2)}) async-start(), calls=%async_computation | async-start | bytes 2097152 | tf_op jit(solution)/shard_map/psum | solution.py:94
  8.6 9.9 %copy-start.3 = (bf16[128,2048]{1,0:T(8,128)(2,1)}, bf16[128,2048]{1,0:T(8,128)(2,1)S(1)}, u32[]{:S(2)}) copy-start(bf16[128,2048]{1,0:T(8,128)(2,1)S(1)} %get-tuple-element.378) | copy-start | bytes 1572868
  8.6 11.5 %collective-permute-start.1 = (bf16[127,2048]{1,0:T(8,128)(2,1)S(1)}, bf16[127,2048]{1,0:T(8,128)(2,1)}, u32[]{:S(2)}, u32[]{:S(2)}) collective-permute-start(bf16[127,2048]{1,0:T(8,128)(2,1)S(1)} %bitcast.171), channel_id=1, source_target_pairs={{1,0},{2,1},{3,2},{4,3},{5,4},{6,5},{7,6},{8,7},{9,8},{10,9},{11,1... | collective-permute-start | bytes 1560584 | tf_op jit(solution)/shard_map/ppermute | solution.py:14
  66.0 2.1 copy-start
  66.2 8.0 %collective-permute-start = (bf16[127,2048]{1,0:T(8,128)(2,1)S(1)}, bf16[127,2048]{1,0:T(8,128)(2,1)}, u32[]{:S(2)}, u32[]{:S(2)}) collective-permute-start(bf16[127,2048]{1,0:T(8,128)(2,1)S(1)} %slice.776), channel_id=1, source_target_pairs={{0,1},{1,2},{2,3},{3,4},{4,5},{5,6},{6,7},{7,8},{8,9},{9,10},{10,1... | collective-permute-start | bytes 1560584 | tf_op jit(solution)/shard_map/ppermute | solution.py:14
  121.2 42.6 %copy-start.1 = (bf16[1,128,2048]{2,1,0:T(8,128)(2,1)S(1)}, bf16[1,128,2048]{2,1,0:T(8,128)(2,1)}, u32[]{:S(2)}) copy-start(bf16[1,128,2048]{2,1,0:T(8,128)(2,1)} %param.11) | copy-start | bytes 1572868
  121.2 42.6 %copy-start.2 = (bf16[1,128,2048]{2,1,0:T(8,128)(2,1)S(1)}, bf16[1,128,2048]{2,1,0:T(8,128)(2,1)}, u32[]{:S(2)}) copy-start(bf16[1,128,2048]{2,1,0:T(8,128)(2,1)} %param.14) | copy-start | bytes 1572868
Sparse Core Ops, SparseCore 0:
  121.3 280.9 all-reduce.1
where the time goes:
time: 412 us; the launch traced here: 411 us
  waiting for transfers between devices  245 us (59%)
  other arithmetic  99.6 us (24%)
  local copies, waits for them, and re-layouts  40.1 us (10%)
  between operations  14.2 us (3%)
  starting transfers between devices  10.7 us (3%)
    psum x1, waiting for transfers between devices, per_device(): summed = lax.psum(partial_sum, ('dp', 'ctx'))  237 us
    reduce_sum x8, other arithmetic, lag_advance(): jnp.sum(grad_float * window[start_row:start_row + length], axis=0)  34.7 us
    add x8, other arithmetic, forward_advance(): running = running + coeffs[inner] * window[start_row:start_row + length]  27.7 us
    add x8, other arithmetic, backward_advance(): running = running + coeffs[inner] * window[inner:inner + length]  27.2 us
    slice x8, local copies, waits for them, and re-layouts, forward_advance(): running = running + coeffs[inner] * window[start_row:start_row + length]  14.4 us
    slice x8, local copies, waits for them, and re-layouts, backward_advance(): running = running + coeffs[inner] * window[inner:inner + length]  14.4 us
    ppermute x2, starting transfers between devices, from_behind(): return lax.ppermute(array, axis, pairs)  10.7 us
  transfers between devices with their start and end apart: 3, of which 3 were waited for; matrix products, arithmetic and copies ran while one was open for 11% of the time, Pallas kernels for 0%

commit v1 on v0

v1 whole, which is shorter than its diff:
```python
import functools
import math

import jax
import jax.numpy as jnp
import ml_dtypes
import numpy as np
from jax import lax
from jax.experimental import pallas as pl
from jax.experimental.pallas import tpu as pltpu
from jax.sharding import PartitionSpec as P

MESH = pl.DeviceIdType.MESH
bf16 = jnp.bfloat16
f32 = jnp.float32
T = 128
F = 128
W = 128
NX = 4


def split(matrix):
    hi = matrix.astype(ml_dtypes.bfloat16)
    lo = (matrix - hi.astype(np.float64)).astype(ml_dtypes.bfloat16)
    return hi, lo


def transforms():
    theta = np.pi * (2 * np.arange(F) + 1) / 256.0
    n = np.arange(T)

    def forward(shift):
        angle = theta[:, None] * (n + shift)[None, :]
        return np.concatenate([np.cos(angle), -np.sin(angle)], axis=0)

    own_hi, own_lo = split(forward(0))
    prev_hi, prev_lo = split(forward(-T))
    back_hi, back_lo = split(forward(0).T / F)
    return (
        np.concatenate([own_hi, own_lo], axis=1),
        np.concatenate([prev_hi, prev_lo], axis=1),
        np.concatenate([back_hi, back_hi, back_lo], axis=1),
    )


def kernel(
    nz, ny,
    q_hbm, k_hbm, v_hbm, g_hbm, h_hbm, own_hbm, prev_hbm, back_hbm,
    y_ref, gq_ref, gk_ref, gv_ref, gf_ref,
    q_ref, k_ref, v_ref, g_ref, h_ref, own_ref, prev_ref, back_ref,
    prev_k, prev_g, kg, halo, extra, spec_k, spec_g, spec_h,
    part, recv1, part2, recv2, part3, recv3,
    load_sem, halo_send, halo_recv, late_recv, extra_send, extra_recv,
    send1, sem1, send2, sem2, send3, sem3,
):
    z = lax.axis_index("dp")
    c = lax.axis_index("ctx")
    nc = ny * 2 * NX
    yy = c // (2 * NX)
    x = (c // 2) % NX
    core = c % 2
    near = 1 - core
    right = {"dp": z, "ctx": lax.rem(c + 1, nc)}
    left = {"dp": z, "ctx": lax.rem(c + nc - 1, nc)}
    partner = {"dp": z, "ctx": c + 1 - 2 * core}

    def at_y(d):
        return {"dp": z, "ctx": lax.rem(yy + d, ny) * (2 * NX) + x * 2 + core}

    def at_z(d):
        return {"dp": lax.rem(z + d, nz), "ctx": c}

    def at_x(xs, ks):
        return {"dp": z, "ctx": yy * (2 * NX) + xs * 2 + ks}

    loads = [
        pltpu.make_async_copy(src, dst, load_sem.at[i])
        for i, (src, dst) in enumerate([
            (k_hbm.at[0], k_ref), (v_hbm.at[0], v_ref), (q_hbm.at[0], q_ref), (g_hbm.at[0], g_ref),
            (own_hbm, own_ref), (prev_hbm, prev_ref), (back_hbm, back_ref), (h_hbm, h_ref),
        ])
    ]
    for copy in loads:
        copy.start()

    barrier = pltpu.get_barrier_semaphore()

    def greet(device):
        pl.semaphore_signal(barrier, inc=1, device_id=device, device_id_type=MESH)

    greet(left)
    greet(right)
    for d in range(1, ny):
        greet(at_y(d))
    for d in range(1, nz):
        greet(at_z(d))
    source_core = x // 2
    for xs in range(NX):
        @pl.when(jnp.logical_or(xs != x, source_core != core))
        def _():
            greet(at_x(xs, source_core))

    def columns(s, b):
        return pl.ds(pl.multiple_of(b * (2 * W) + s * W, W), W)

    def products(s):
        def step(b, carry):
            cols = columns(s, b)
            kg[0, s, b] = (k_ref[:, cols].astype(f32) * v_ref[:, cols].astype(f32)).astype(bf16)
            kg[1, s, b] = (g_ref[:, cols].astype(f32) * q_ref[:, cols].astype(f32)).astype(bf16)
            return carry

        lax.fori_loop(0, ny, step, 0)

    for copy in loads[:4]:
        copy.wait()
    products(near)
    targets = jnp.where(source_core == core, 3, 4)
    pl.semaphore_wait(barrier, 2 + (ny - 1) + (nz - 1) + targets)

    def halo_copy(array, s, b, device):
        return pltpu.make_async_remote_copy(
            src_ref=kg.at[array, s, b], dst_ref=halo.at[array, s, b],
            send_sem=halo_send.at[array], recv_sem=halo_recv.at[array, b],
            device_id=device, device_id_type=MESH,
        )

    def late_copy(array, device):
        return pltpu.make_async_remote_copy(
            src_ref=kg.at[array, core], dst_ref=halo.at[array, core],
            send_sem=halo_send.at[array], recv_sem=late_recv.at[array],
            device_id=device, device_id_type=MESH,
        )

    def extra_copy(b):
        return pltpu.make_async_remote_copy(
            src_ref=kg.at[near, near, b], dst_ref=extra.at[b],
            send_sem=extra_send, recv_sem=extra_recv.at[b],
            device_id=partner, device_id_type=MESH,
        )

    def early(i, carry):
        b = lax.rem(yy + 1 + i, ny)
        halo_copy(0, near, b, right).start()
        halo_copy(1, near, b, left).start()
        extra_copy(b).start()
        return carry

    lax.fori_loop(0, ny, early, 0)
    products(core)

    for copy in loads[4:]:
        copy.wait()
    prev_k[...] = prev_ref[...] * jnp.where(c > 0, 1.0, 0.0).astype(bf16)
    prev_g[...] = prev_ref[...] * jnp.where(c < nc - 1, -1.0, 0.0).astype(bf16)

    def twice(value):
        return jnp.concatenate([value, value], axis=0)

    def forward(matrix, value):
        return jnp.dot(matrix, twice(value), preferred_element_type=f32)

    def pair(ref, *index):
        *lead, b0, b1 = index
        return jnp.concatenate([ref[(*lead, b0)], ref[(*lead, b1)]], axis=1)

    def put(ref, s, b0, b1, value):
        ref[s, b0] = value[:, :W]
        ref[s, b1] = value[:, W:]

    def own_spectra(s):
        def step(i, carry):
            b0, b1 = 2 * i, 2 * i + 1
            put(spec_k, s, b0, b1, forward(own_ref[...], pair(kg, 0, s, b0, b1)))
            put(spec_g, s, b0, b1, forward(own_ref[...], pair(kg, 1, s, b0, b1)))
            taps = jnp.concatenate([h_ref[:, columns(s, b0)], h_ref[:, columns(s, b1)]], axis=1)
            put(spec_h, s, b0, b1, forward(own_ref[...], taps))
            return carry

        lax.fori_loop(0, ny // 2, step, 0)

    own_spectra(core)
    own_spectra(near)

    def times(a, b):
        ar, ai, br, bi = a[:F], a[F:], b[:F], b[F:]
        return ar * br - ai * bi, ar * bi + ai * br

    def times_conj(a, b):
        ar, ai, br, bi = a[:F], a[F:], b[:F], b[F:]
        return ar * br + ai * bi, ai * br - ar * bi

    def inverse(re, im):
        value = jnp.concatenate([re, im], axis=0)
        hi = value.astype(bf16)
        lo = (value - hi.astype(f32)).astype(bf16)
        return jnp.dot(
            back_ref[...], jnp.concatenate([hi, lo, hi], axis=0), preferred_element_type=f32
        )

    def gradient(i, carry):
        b0 = lax.rem(yy + 1 + 2 * i, ny)
        b1 = lax.rem(yy + 2 + 2 * i, ny)
        for b in (b0, b1):
            halo_copy(0, core, b, right).wait_recv()
            halo_copy(1, core, b, left).wait_recv()
            extra_copy(b).wait_recv()
        own_k = pair(spec_k, core, b0, b1)
        own_g = pair(spec_g, core, b0, b1)
        k_prev = forward(prev_k[...], pair(halo, 0, core, b0, b1))
        g_next = forward(prev_g[...], pair(halo, 1, core, b0, b1))
        other = forward(prev_ref[...], pair(extra, b0, b1))
        g_all = own_g + g_next
        put(spec_k, core, b0, b1, own_k + k_prev)
        put(spec_g, core, b0, b1, g_all)
        first = core == 0
        u = jnp.where(first, -g_next, other)
        w = jnp.where(first, other, k_prev)
        re0, im0 = times_conj(g_all, own_k)
        re1, im1 = times_conj(own_g, k_prev)
        re2, im2 = times_conj(u, w)
        value = inverse(re0 + re1 + re2, im0 + im1 + im2).astype(bf16)
        part[b0] = value[:, :W]
        part[b1] = value[:, W:]

        def send(d, b):
            pltpu.make_async_remote_copy(
                src_ref=part.at[b], dst_ref=recv1.at[d - 1], send_sem=send1, recv_sem=sem1,
                device_id=at_y(d), device_id_type=MESH,
            ).start()

        send(1 + 2 * i, b0)

        @pl.when(i < ny // 2 - 1)
        def _():
            send(2 + 2 * i, b1)

        return carry

    late_copy(0, right).start()
    late_copy(1, left).start()
    lax.fori_loop(0, ny // 2, gradient, 0)

    def outputs(s):
        def step(i, carry):
            b0, b1 = 2 * i, 2 * i + 1
            k_all = pair(spec_k, s, b0, b1)
            g_all = pair(spec_g, s, b0, b1)
            if s is near:
                k_all += forward(prev_k[...], pair(halo, 0, s, b0, b1))
                g_all += forward(prev_g[...], pair(halo, 1, s, b0, b1))
            taps = pair(spec_h, s, b0, b1)
            mixed = inverse(*times(k_all, taps))
            flowing = inverse(*times_conj(g_all, taps))
            for at, b in enumerate((b0, b1)):
                cols = columns(s, b)
                m = mixed[:, at * W:(at + 1) * W]
                y_ref[0, :, cols] = (q_ref[:, cols].astype(f32) * m).astype(bf16)
                gq_ref[0, :, cols] = (g_ref[:, cols].astype(f32) * m).astype(bf16)
                m = flowing[:, at * W:(at + 1) * W]
                gk_ref[0, :, cols] = (v_ref[:, cols].astype(f32) * m).astype(bf16)
                gv_ref[0, :, cols] = (k_ref[:, cols].astype(f32) * m).astype(bf16)
            return carry

        lax.fori_loop(0, ny // 2, step, 0)

    outputs(core)

    def late_arrival(array, device):
        return pltpu.make_async_remote_copy(
            src_ref=kg.at[array, near], dst_ref=halo.at[array, near],
            send_sem=halo_send.at[array], recv_sem=late_recv.at[array],
            device_id=device, device_id_type=MESH,
        )

    late_arrival(0, right).wait_recv()
    late_arrival(1, left).wait_recv()
    outputs(near)

    def landed(ref, sem):
        pltpu.make_async_copy(ref, ref, sem).wait()

    landed(recv1, sem1)
    total = part[yy].astype(f32)
    for d in range(ny - 1):
        total += recv1[d].astype(f32)
    part2[...] = jnp.transpose(total).astype(bf16).reshape(4, 32, T)
    for r in range(2):
        for ks in range(2):
            xs = 2 * core + r

            @pl.when(jnp.logical_or(xs != x, ks != core))
            def _():
                pltpu.make_async_remote_copy(
                    src_ref=part2.at[r * 2 + ks], dst_ref=recv2.at[x], send_sem=send2, recv_sem=sem2.at[x],
                    device_id=at_x(xs, ks), device_id_type=MESH,
                ).start()

            @pl.when(jnp.logical_not(jnp.logical_or(xs != x, ks != core)))
            def _():
                recv2[x] = part2[r * 2 + ks]
    for xs in range(NX):
        @pl.when(jnp.logical_or(xs != x, source_core != core))
        def _():
            landed(recv2.at[xs], sem2.at[xs])
    total = recv2[0].astype(f32)
    for xs in range(1, NX):
        total += recv2[xs].astype(f32)
    part3[...] = total
    for d in range(1, nz):
        pltpu.make_async_remote_copy(
            src_ref=part3, dst_ref=recv3.at[d - 1], send_sem=send3, recv_sem=sem3,
            device_id=at_z(d), device_id_type=MESH,
        ).start()
    landed(recv3, sem3)
    for d in range(nz - 1):
        total += recv3[d]
    gf_ref[...] = total * (1.0 / math.sqrt(T * nc * nz))

    landed(kg.at[0], halo_send.at[0])
    landed(kg.at[1], halo_send.at[1])
    landed(extra, extra_send)
    landed(recv1, send1)
    landed(part2.at[:3], send2)

    @pl.when(source_core != core)
    def _():
        landed(part2.at[3], send2)

    landed(recv3, send3)


def per_device(query_act, key_act, value_act, grad_out, filter_taps):
    channels = filter_taps.shape[1]
    ny = channels // (2 * W)
    nz = lax.axis_size("dp")
    own, prev, back = transforms()
    big = (1, T, channels)
    any_spec = pl.BlockSpec(memory_space=pl.ANY)
    vmem = pl.BlockSpec(memory_space=pltpu.VMEM)
    dma = pltpu.SemaphoreType.DMA
    outs = pl.pallas_call(
        functools.partial(kernel, nz, ny),
        out_shape=[jax.ShapeDtypeStruct(big, bf16)] * 4 + [jax.ShapeDtypeStruct((32, T), f32)],
        in_specs=[any_spec] * 8,
        out_specs=[vmem] * 5,
        scratch_shapes=[
            *[pltpu.VMEM((T, channels), bf16)] * 5,
            pltpu.VMEM((2 * F, 2 * T), bf16),
            pltpu.VMEM((2 * F, 2 * T), bf16),
            pltpu.VMEM((T, 6 * F), bf16),
            pltpu.VMEM((2 * F, 2 * T), bf16),
            pltpu.VMEM((2 * F, 2 * T), bf16),
            pltpu.VMEM((2, 2, ny, T, W), bf16),
            pltpu.VMEM((2, 2, ny, T, W), bf16),
            pltpu.VMEM((ny, T, W), bf16),
            *[pltpu.VMEM((2, ny, 2 * F, W), f32)] * 3,
            pltpu.VMEM((ny, T, W), bf16),
            pltpu.VMEM((ny - 1, T, W), bf16),
            pltpu.VMEM((4, 32, T), bf16),
            pltpu.VMEM((NX, 32, T), bf16),
            pltpu.VMEM((32, T), f32),
            pltpu.VMEM((nz - 1, 32, T), f32),
            dma((8,)), dma((2,)), dma((2, ny)), dma((2,)), dma(()), dma((ny,)),
            dma(()), dma(()), dma(()), dma((NX,)), dma(()), dma(()),
        ],
        compiler_params=pltpu.CompilerParams(
            collective_id=1, has_side_effects=True, vmem_limit_bytes=60 * 2**20
        ),
    )(query_act, key_act, value_act, grad_out, filter_taps, own, prev, back)
    return (*outs[:4], outs[4].T)


def solution(mesh):
    spread = P("dp", "ctx", None)
    return jax.shard_map(
        per_device, mesh=mesh, in_specs=(spread,) * 4 + (P(),),
        out_specs=(spread,) * 4 + (P(None, "ctx"),), check_vma=False,
    )
```

time: 412 us -> 45 us (0.11)
  waiting for transfers between devices: 245 us -> 0 us
  other arithmetic: 99.6 us -> 0 us
  Pallas kernels: 0 us -> 38.3 us
  local copies, waits for them, and re-layouts: 40.1 us -> 5.8 us
  between operations: 14.2 us -> 0.65 us
  starting transfers between devices: 10.7 us -> 0 us
    psum x1 -> x0, waiting for transfers between devices: 237 us -> none  [per_device(): summed = lax.psum(partial_sum, ('dp', 'ctx'))]
    add x16 -> x0, other arithmetic: 54.9 us -> none  [the longest x8 27.7 us: forward_advance(): running = running + coeffs[inner] * window[start_row:start_row + length]]
    pallas_call x0 -> x1, Pallas kernels: none -> 38.3 us  [per_device(): pl.pallas_call(functools.partial(kernel, nz, ny), out_shape=[jax.ShapeDty...]
    reduce_sum x8 -> x0, other arithmetic: 34.7 us -> none  [lag_advance(): jnp.sum(grad_float * window[start_row:start_row + length], axis=0)]
    slice x17 -> x0, local copies, waits for them, and re-layouts: 29 us -> none  [the longest x8 14.4 us: forward_advance(): running = running + coeffs[inner] * window[start_row:start_row + length]]
    ppermute x2 -> x0, starting transfers between devices: 10.7 us -> none  [from_behind(): return lax.ppermute(array, axis, pairs)]
    ppermute x2 -> x0, waiting for transfers between devices: 7.63 us -> none  [from_behind(): return lax.ppermute(array, axis, pairs)]
    unnamed x10 -> x13, local copies, waits for them, and re-layouts: 0.03 us -> 5.8 us
  transfers between devices with their start and end apart: 3 -> 0, of which waited for: 3 -> 0; matrix products, arithmetic and copies ran while one was open for 11% -> 0% of each run, Pallas kernels for 0% -> 0%
where the time goes in v1:
time: 45 us; the launch traced here: 44.7 us
  Pallas kernels  38.3 us (85%)
  local copies, waits for them, and re-layouts  5.8 us (13%)
  between operations  0.65 us (1%)
    pallas_call x1, Pallas kernels, per_device(): pl.pallas_call(functools.partial(kernel, nz, ny), out_shape=[jax.ShapeDty...  38.3 us
    unnamed x13, local copies, waits for them, and re-layouts  5.8 us

profile of v1, /device:TPU:1, one launch (start us, length us, event | category | flops | bytes accessed | tf_op | source)
XLA Modules:
  0.0 44.7 jit_solution(8724019917743976910)
XLA Ops:
  0.6 38.3 %shard_map.119 = (bf16[1,128,2048]{2,1,0:T(8,128)(2,1)}, bf16[1,128,2048]{2,1,0:T(8,128)(2,1)}, bf16[1,128,2048]{2,1,0:T(8,128)(2,1)}, bf16[1,128,2048]{2,1,0:T(8,128)(2,1)}, f32[32,128]{1,0:T(8,128)}) custom-call(bf16[1,128,2048]{2,1,0:T(8,128)(2,1)} %q_hbm.1, bf16[1,128,2048]{2,1,0:T(8,128)(2,1)} %k_hbm.1, bf16[1,128,2048]{2,1,0:T(8,128)(2,1)} %v_hbm.1, ...), custom_call_target="tpu_custom_call" | custom-call | tf_op jit(solution)/shard_map/pallas_call | solution.py:342
  38.9 0.0 copy-start.2
  38.9 1.9 %copy.18 = bf16[1,128,2048]{2,1,0:T(8,128)(2,1)} copy(bf16[1,128,2048]{2,1,0:T(8,128)(2,1)} %get-tuple-element.20) | data formatting | bytes 1048576
  40.9 0.0 copy-done.2
  40.9 0.0 copy-start.1
  40.9 0.8 %copy.19 = bf16[1,128,2048]{2,1,0:T(8,128)(2,1)} copy(bf16[1,128,2048]{2,1,0:T(8,128)(2,1)S(1)} %copy-done.2) | data formatting | bytes 1048576
  41.7 0.4 copy-done.1
  42.1 0.0 copy-start
  42.1 0.8 %copy.20 = bf16[1,128,2048]{2,1,0:T(8,128)(2,1)} copy(bf16[1,128,2048]{2,1,0:T(8,128)(2,1)S(1)} %copy-done.1) | data formatting | bytes 1048576
  42.9 0.4 copy-done
  43.3 0.0 copy-start.3
  43.3 0.8 %copy.21 = bf16[1,128,2048]{2,1,0:T(8,128)(2,1)} copy(bf16[1,128,2048]{2,1,0:T(8,128)(2,1)S(1)} %copy-done) | data formatting | bytes 1048576
  44.1 0.0 copy-done.3
  44.1 0.6 %copy.22 = f32[128,32]{0,1:T(8,128)} copy(f32[128,32]{0,1:T(8,128)S(1)} %bitcast.1) | data formatting | bytes 32768
Async XLA Ops:
  38.9 2.0 %copy-start.2 = (bf16[1,128,2048]{2,1,0:T(8,128)(2,1)S(1)}, bf16[1,128,2048]{2,1,0:T(8,128)(2,1)}, u32[]{:S(2)}) copy-start(bf16[1,128,2048]{2,1,0:T(8,128)(2,1)} %get-tuple-element.21) | copy-start | bytes 1572868
  40.9 1.2 %copy-start.1 = (bf16[1,128,2048]{2,1,0:T(8,128)(2,1)S(1)}, bf16[1,128,2048]{2,1,0:T(8,128)(2,1)}, u32[]{:S(2)}) copy-start(bf16[1,128,2048]{2,1,0:T(8,128)(2,1)} %get-tuple-element.22) | copy-start | bytes 1572868
  42.1 1.2 %copy-start = (bf16[1,128,2048]{2,1,0:T(8,128)(2,1)S(1)}, bf16[1,128,2048]{2,1,0:T(8,128)(2,1)}, u32[]{:S(2)}) copy-start(bf16[1,128,2048]{2,1,0:T(8,128)(2,1)} %get-tuple-element.23) | copy-start | bytes 1572868
  43.3 0.8 %copy-start.3 = (f32[32,128]{1,0:T(8,128)S(1)}, f32[32,128]{1,0:T(8,128)}, u32[]{:S(2)}) copy-start(f32[32,128]{1,0:T(8,128)} %get-tuple-element.14) | copy-start | bytes 49156

commit v2 on v1

v2 whole, which is shorter than its diff:
```python
import functools
import math

import jax
import jax.numpy as jnp
import ml_dtypes
import numpy as np
from jax import lax
from jax.experimental import pallas as pl
from jax.experimental.pallas import tpu as pltpu
from jax.sharding import PartitionSpec as P

MESH = pl.DeviceIdType.MESH
bf16 = jnp.bfloat16
f32 = jnp.float32
T = 128
F = 128
W = 256
NX = 4
VMEM_BYTES = 62 * 2**20
PIECES = 2


def split(matrix):
    hi = matrix.astype(ml_dtypes.bfloat16)
    lo = (matrix - hi.astype(np.float64)).astype(ml_dtypes.bfloat16)
    return hi, lo


def transforms():
    theta = np.pi * (2 * np.arange(F) + 1) / 256.0
    n = np.arange(T)

    def forward(shift):
        angle = theta[:, None] * (n + shift)[None, :]
        return np.concatenate([np.cos(angle), -np.sin(angle)], axis=0)

    own_hi, own_lo = split(forward(0))
    prev_hi, prev_lo = split(forward(-T))
    back_hi, back_lo = split(forward(0).T / F)
    return (
        np.concatenate([own_hi, own_lo], axis=1),
        np.concatenate([prev_hi, prev_lo], axis=1),
        np.concatenate([back_hi, back_hi, back_lo], axis=1),
    )


def kernel(
    nz, ny,
    q_hbm, k_hbm, v_hbm, g_hbm, h_hbm, own_hbm, prev_hbm, back_hbm,
    y_hbm, gq_hbm, gk_hbm, gv_hbm, gf_ref,
    q_ref, k_ref, v_ref, g_ref, h_ref, own_ref, prev_ref, back_ref,
    prev_kg, kg, halo, extra, spec, spec_h, early_sum, mates,
    part_x, recv_x, part_y, recv_y, part_z, recv_z,
    load_sem, const_sem, out_sem, halo_send, halo_recv, late_recv, extra_send, extra_recv,
    send_x, sem_x, send_y, sem_y, send_z, sem_z,
):
    z = lax.axis_index("dp")
    c = lax.axis_index("ctx")
    nc = ny * 2 * NX
    yy = c // (2 * NX)
    x = (c // 2) % NX
    core = c % 2
    near = 1 - core
    nb = ny // 2
    half = nb * W
    right = {"dp": z, "ctx": lax.rem(c + 1, nc)}
    left = {"dp": z, "ctx": lax.rem(c + nc - 1, nc)}
    partner = {"dp": z, "ctx": c + 1 - 2 * core}

    def at(y_to, x_to, core_to):
        return {"dp": z, "ctx": y_to * (2 * NX) + x_to * 2 + core_to}

    def at_x(d):
        return at(yy, lax.rem(x + d, NX), core)

    def at_z(d):
        return {"dp": lax.rem(z + d, nz), "ctx": c}

    def load(s):
        cols = pl.ds(pl.multiple_of(s * half, half), half)
        return [
            pltpu.make_async_copy(src.at[0, :, cols], dst.at[s], load_sem.at[s, i])
            for i, (src, dst) in enumerate(
                [(k_hbm, k_ref), (v_hbm, v_ref), (g_hbm, g_ref), (q_hbm, q_ref)]
            )
        ]

    for copy in load(near):
        copy.start()
    constants = [
        pltpu.make_async_copy(src, dst, const_sem.at[i])
        for i, (src, dst) in enumerate(
            [(own_hbm, own_ref), (h_hbm, h_ref), (prev_hbm, prev_ref), (back_hbm, back_ref)]
        )
    ]
    barrier = pltpu.get_barrier_semaphore()

    def greet(device):
        pl.semaphore_signal(barrier, inc=1, device_id=device, device_id_type=MESH)

    greet(left)
    greet(right)
    for d in range(1, NX):
        greet(at_x(d))
    for d in range(1, nz):
        greet(at_z(d))
    source_core = yy // nb
    own_source = source_core == core
    for ys in range(ny):
        @pl.when(jnp.logical_not(jnp.logical_and(ys == yy, own_source)))
        def _():
            greet(at(ys, x, source_core))

    def products(s):
        for j in range(nb):
            cols = slice(j * W, (j + 1) * W)
            b = s * nb + j
            kg[0, b] = (k_ref[s, :, cols].astype(f32) * v_ref[s, :, cols].astype(f32)).astype(bf16)
            kg[1, b] = (g_ref[s, :, cols].astype(f32) * q_ref[s, :, cols].astype(f32)).astype(bf16)

    for copy in load(near):
        copy.wait()
    for copy in load(core):
        copy.start()
    for copy in constants:
        copy.start()
    products(near)
    pl.semaphore_wait(barrier, 2 + (NX - 1) + (nz - 1) + jnp.where(own_source, ny - 1, ny))

    def halo_copy(array, b, device):
        return pltpu.make_async_remote_copy(
            src_ref=kg.at[array, b], dst_ref=halo.at[array, b],
            send_sem=halo_send.at[array], recv_sem=halo_recv.at[array, b % nb],
            device_id=device, device_id_type=MESH,
        )

    def late_copy(array, s, device):
        return pltpu.make_async_remote_copy(
            src_ref=kg.at[array, pl.ds(s * nb, nb)], dst_ref=halo.at[array, pl.ds(s * nb, nb)],
            send_sem=halo_send.at[array], recv_sem=late_recv.at[array],
            device_id=device, device_id_type=MESH,
        )

    def extra_copy(j):
        return pltpu.make_async_remote_copy(
            src_ref=kg.at[near, near * nb + j], dst_ref=extra.at[j],
            send_sem=extra_send, recv_sem=extra_recv.at[j],
            device_id=partner, device_id_type=MESH,
        )

    for j in range(nb):
        halo_copy(0, near * nb + j, right).start()
        halo_copy(1, near * nb + j, left).start()
        extra_copy(j).start()

    for copy in load(core):
        copy.wait()
    products(core)

    for copy in constants:
        copy.wait()
    prev_kg[0] = prev_ref[...] * jnp.where(c > 0, 1.0, 0.0).astype(bf16)
    prev_kg[1] = prev_ref[...] * jnp.where(c < nc - 1, -1.0, 0.0).astype(bf16)

    def forward(matrix, value):
        return jnp.dot(
            matrix, jnp.concatenate([value, value], axis=0), preferred_element_type=f32
        )

    def own_spectra(s):
        def step(j, carry):
            b = s * nb + j
            spec[0, b] = forward(own_ref[...], kg[0, b])
            spec[1, b] = forward(own_ref[...], kg[1, b])
            taps = h_ref[:, pl.ds(pl.multiple_of(b * W, W), W)]
            spec_h[b] = forward(own_ref[...], taps)
            return carry

        lax.fori_loop(0, nb, step, 0)

    own_spectra(core)
    own_spectra(near)

    def times(a, b):
        ar, ai, br, bi = a[:F], a[F:], b[:F], b[F:]
        return ar * br - ai * bi, ar * bi + ai * br

    def times_conj(a, b):
        ar, ai, br, bi = a[:F], a[F:], b[:F], b[F:]
        return ar * br + ai * bi, ai * br - ar * bi

    def inverse(re, im):
        value = jnp.concatenate([re, im], axis=0)
        hi = value.astype(bf16)
        lo = (value - hi.astype(f32)).astype(bf16)
        return jnp.dot(
            back_ref[...], jnp.concatenate([hi, lo, hi], axis=0), preferred_element_type=f32
        )

    first = core == 0

    def early_terms(j, carry):
        b = core * nb + j
        halo_copy(1 - core, b, partner).wait_recv()
        extra_copy(j).wait_recv()
        fast = forward(prev_kg[near], halo[near, b])
        other = forward(prev_ref[...], extra[j])
        own_k = spec[0, b]
        own_g = spec[1, b]
        spec[near, b] = spec[near, b] + fast
        re0, im0 = times_conj(jnp.where(first, own_g + fast, own_g), jnp.where(first, own_k, own_k + fast))
        re1, im1 = times_conj(jnp.where(first, -fast, other), jnp.where(first, other, fast))
        mates[j] = jnp.where(first, own_g, own_k)
        early_sum[j, :F] = re0 + re1
        early_sum[j, F:] = im0 + im1
        return carry

    lax.fori_loop(0, nb, early_terms, 0)

    def gradient(j, carry):
        b = core * nb + j
        halo_copy(core, b, partner).wait_recv()
        slow = forward(prev_kg[core], halo[core, b])
        own = spec[core, b]
        spec[core, b] = own + slow
        mate = mates[j]
        re, im = times_conj(jnp.where(first, mate, slow), jnp.where(first, slow, mate))
        value = inverse(early_sum[j, :F] + re, early_sum[j, F:] + im)
        part_x[j] = jnp.transpose(value).astype(bf16).reshape(NX, W // NX, T)
        for d in range(1, NX):
            pltpu.make_async_remote_copy(
                src_ref=part_x.at[j, lax.rem(x + d, NX)], dst_ref=recv_x.at[d - 1, j],
                send_sem=send_x, recv_sem=sem_x, device_id=at_x(d), device_id_type=MESH,
            ).start()
        return carry

    lax.fori_loop(0, nb, gradient, 0)
    late_copy(0, core, right).start()
    late_copy(1, core, left).start()

    def outputs(s):
        def step(j, carry):
            b = s * nb + j
            k_all = spec[0, b]
            g_all = spec[1, b]
            if s is near:
                k_all += forward(prev_kg[0], halo[0, b])
                g_all += forward(prev_kg[1], halo[1, b])
            taps = spec_h[b]
            cols = pl.ds(pl.multiple_of(j * W, W), W)
            m = inverse(*times(k_all, taps))
            q_ref[s, :, cols] = (q_ref[s, :, cols].astype(f32) * m).astype(bf16)
            g_ref[s, :, cols] = (g_ref[s, :, cols].astype(f32) * m).astype(bf16)
            m = inverse(*times_conj(g_all, taps))
            v_ref[s, :, cols] = (v_ref[s, :, cols].astype(f32) * m).astype(bf16)
            k_ref[s, :, cols] = (k_ref[s, :, cols].astype(f32) * m).astype(bf16)
            return carry

        lax.fori_loop(0, nb, step, 0)

    def store(s):
        cols = pl.ds(pl.multiple_of(s * half, half), half)
        return [
            pltpu.make_async_copy(src.at[s], dst.at[0, :, cols], out_sem.at[s, i])
            for i, (src, dst) in enumerate(
                [(q_ref, y_hbm), (g_ref, gq_hbm), (v_ref, gk_hbm), (k_ref, gv_hbm)]
            )
        ]

    def landed(ref, sem):
        pltpu.make_async_copy(ref, ref, sem).wait()

    outputs(core)
    for copy in store(core):
        copy.start()

    landed(recv_x, sem_x)
    for j in range(nb):
        total = part_x[j, x].astype(f32)
        for d in range(NX - 1):
            total += recv_x[d, j].astype(f32)
        part_y[j] = total.astype(bf16).reshape(2, W // NX // 2, T)
        for core_to in range(2):
            mine = jnp.logical_and(jnp.logical_and(own_source, yy == core * nb + j), core == core_to)

            @pl.when(jnp.logical_not(mine))
            def _():
                pltpu.make_async_remote_copy(
                    src_ref=part_y.at[j, core_to], dst_ref=recv_y.at[yy],
                    send_sem=send_y, recv_sem=sem_y.at[yy],
                    device_id=at(core * nb + j, x, core_to), device_id_type=MESH,
                ).start()

            @pl.when(mine)
            def _():
                recv_y[yy] = part_y[j, core_to]

    for ys in range(ny):
        @pl.when(jnp.logical_not(jnp.logical_and(ys == yy, own_source)))
        def _():
            landed(recv_y.at[ys], sem_y.at[ys])
    total = recv_y[0].astype(f32)
    for ys in range(1, ny):
        total += recv_y[ys].astype(f32)
    part_z[...] = total.astype(bf16)
    for d in range(1, nz):
        pltpu.make_async_remote_copy(
            src_ref=part_z, dst_ref=recv_z.at[d - 1], send_sem=send_z, recv_sem=sem_z,
            device_id=at_z(d), device_id_type=MESH,
        ).start()

    late_copy(0, near, right).wait_recv()
    late_copy(1, near, left).wait_recv()
    outputs(near)
    for copy in store(near):
        copy.start()

    landed(recv_z, sem_z)
    total = part_z[...].astype(f32)
    for d in range(nz - 1):
        total += recv_z[d].astype(f32)
    gf_ref[...] = total * (1.0 / math.sqrt(T * nc * nz))

    landed(kg.at[0], halo_send.at[0])
    landed(kg.at[1], halo_send.at[1])
    landed(extra, extra_send)
    landed(recv_x, send_x)
    landed(recv_y.at[pl.ds(0, ny - 1)], send_y)

    @pl.when(jnp.logical_not(own_source))
    def _():
        landed(recv_y.at[ny - 1], send_y)

    landed(recv_z, send_z)

    for s in (core, near):
        for copy in store(s):
            copy.wait()


def write_out(*refs):
    sources, targets, held, (load_sem, store_sem) = refs[:5], refs[5:10], refs[10:15], refs[15:]
    rows = T // PIECES
    loads, stores = [], []
    for i in range(5):
        for piece in range(PIECES if i < 4 else 1):
            at = (0, pl.ds(piece * rows, rows)) if i < 4 else ()
            loads.append(pltpu.make_async_copy(
                sources[i].at[at], held[i].at[at], load_sem.at[i, piece]))
            stores.append(pltpu.make_async_copy(
                held[i].at[at], targets[i].at[at], store_sem.at[i, piece]))
    for load in loads:
        load.start()
    for load, store in zip(loads, stores):
        load.wait()
        store.start()
    for store in stores:
        store.wait()


def per_device(query_act, key_act, value_act, grad_out, filter_taps):
    channels = filter_taps.shape[1]
    ny = channels // W
    nz = lax.axis_size("dp")
    own, prev, back = transforms()
    big = jax.ShapeDtypeStruct((1, T, channels), bf16)
    half = channels // 2
    cols = W // NX // 2
    small = jax.ShapeDtypeStruct((cols, T), f32)
    hbm = pl.BlockSpec(memory_space=pl.ANY)
    vmem = pl.BlockSpec(memory_space=pltpu.VMEM)
    dma = pltpu.SemaphoreType.DMA
    limit = VMEM_BYTES
    outs = pl.pallas_call(
        functools.partial(kernel, nz, ny),
        out_shape=[big] * 4 + [small],
        in_specs=[hbm] * 8,
        out_specs=[hbm] * 4 + [vmem],
        scratch_shapes=[
            *[pltpu.VMEM((2, T, half), bf16)] * 4,
            pltpu.VMEM((T, channels), bf16),
            pltpu.VMEM((2 * F, 2 * T), bf16),
            pltpu.VMEM((2 * F, 2 * T), bf16),
            pltpu.VMEM((T, 6 * F), bf16),
            pltpu.VMEM((2, 2 * F, 2 * T), bf16),
            pltpu.VMEM((2, ny, T, W), bf16),
            pltpu.VMEM((2, ny, T, W), bf16),
            pltpu.VMEM((ny // 2, T, W), bf16),
            pltpu.VMEM((2, ny, 2 * F, W), f32),
            pltpu.VMEM((ny, 2 * F, W), f32),
            pltpu.VMEM((ny // 2, 2 * F, W), f32),
            pltpu.VMEM((ny // 2, 2 * F, W), f32),
            pltpu.VMEM((ny // 2, NX, W // NX, T), bf16),
            pltpu.VMEM((NX - 1, ny // 2, W // NX, T), bf16),
            pltpu.VMEM((ny // 2, 2, cols, T), bf16),
            pltpu.VMEM((ny, cols, T), bf16),
            pltpu.VMEM((cols, T), bf16),
            pltpu.VMEM((nz - 1, cols, T), bf16),
            dma((2, 4)), dma((4,)), dma((2, 4)), dma((2,)), dma((2, ny // 2)), dma((2,)),
            dma(()), dma((ny // 2,)), dma(()), dma(()), dma(()), dma((ny,)), dma(()), dma(()),
        ],
        compiler_params=pltpu.CompilerParams(
            collective_id=1, has_side_effects=True, vmem_limit_bytes=limit
        ),
    )(query_act, key_act, value_act, grad_out, filter_taps, own, prev, back)
    *done, summed = pl.pallas_call(
        write_out,
        out_shape=[big] * 4 + [small],
        in_specs=[hbm] * 5,
        out_specs=[hbm] * 5,
        scratch_shapes=[pltpu.VMEM(big.shape, bf16)] * 4 + [pltpu.VMEM(small.shape, f32)] + [dma((5, PIECES))] * 2,
        compiler_params=pltpu.CompilerParams(vmem_limit_bytes=limit),
    )(*outs)
    return (*done, summed.T)


def solution(mesh):
    spread = P("dp", "ctx", None)
    return jax.shard_map(
        per_device, mesh=mesh, in_specs=(spread,) * 4 + (P(),),
        out_specs=(spread,) * 4 + (P(None, "ctx"),), check_vma=False,
    )
```

time: 45 us -> 40.2 us (0.89)
  local copies, waits for them, and re-layouts: 5.8 us -> 0 us
  Pallas kernels: 38.3 us -> 39.4 us
    unnamed x13 -> x0, local copies, waits for them, and re-layouts: 5.8 us -> none
    pallas_call x1 -> x2, Pallas kernels: 38.3 us -> 39.4 us  [the longest x1 37 us: per_device(): pl.pallas_call(functools.partial(kernel, nz, ny), out_shape=[big] * 4 + [...]
where the time goes in v2:
time: 40.2 us; the launch traced here: 40.1 us
  Pallas kernels  39.4 us (98%)
  between operations  0.64 us (2%)
    pallas_call x1, Pallas kernels, per_device(): pl.pallas_call(functools.partial(kernel, nz, ny), out_shape=[big] * 4 + [...  37 us
    pallas_call x1, Pallas kernels, per_device(): pl.pallas_call(write_out, out_shape=[big] * 4 + [small], in_specs=[hbm] *...  2.43 us

profile of v2, /device:TPU:1, one launch (start us, length us, event | category | flops | bytes accessed | tf_op | source)
XLA Modules:
  0.0 40.1 jit_solution(16618968998307849321)
XLA Ops:
  0.6 37.0 %shard_map.119 = (bf16[1,128,2048]{2,1,0:T(8,128)(2,1)}, bf16[1,128,2048]{2,1,0:T(8,128)(2,1)}, bf16[1,128,2048]{2,1,0:T(8,128)(2,1)}, bf16[1,128,2048]{2,1,0:T(8,128)(2,1)}, f32[32,128]{1,0:T(8,128)}) custom-call(bf16[1,128,2048]{2,1,0:T(8,128)(2,1)} %q_hbm.1, bf16[1,128,2048]{2,1,0:T(8,128)(2,1)} %k_hbm.1, bf16[1,128,2048]{2,1,0:T(8,128)(2,1)} %v_hbm.1, ...), custom_call_target="tpu_custom_call" | custom-call | tf_op jit(solution)/shard_map/pallas_call | solution.py:375
  37.6 2.4 %shard_map.120 = (bf16[1,128,2048]{2,1,0:T(8,128)(2,1)}, bf16[1,128,2048]{2,1,0:T(8,128)(2,1)}, bf16[1,128,2048]{2,1,0:T(8,128)(2,1)}, bf16[1,128,2048]{2,1,0:T(8,128)(2,1)}, f32[32,128]{1,0:T(8,128)}) custom-call(bf16[1,128,2048]{2,1,0:T(8,128)(2,1)} %get-tuple-element.15.refs_0_, bf16[1,128,2048]{2,1,0:T(8,128)(2,1)} %get-tuple-element.16.refs_1_, ...), custom_call_target="tpu_custom_call" | custom-call | tf_op jit(solution)/shard_map/pallas_call | solution.py:407

commit v3 on v2

--- a/solution.py
+++ b/solution.py
@@ -17,7 +17,10 @@
 F = 128
 W = 256
 NX = 4
-VMEM_BYTES = 62 * 2**20
+VMEM_BYTES = 64929792
+PIECES = 2
+PIECES = 2
+PIECES = 2
 PIECES = 2
 
 
@@ -52,7 +55,7 @@
     q_ref, k_ref, v_ref, g_ref, h_ref, own_ref, prev_ref, back_ref,
     prev_kg, kg, halo, extra, spec, spec_h, early_sum, mates,
     part_x, recv_x, part_y, recv_y, part_z, recv_z,
-    load_sem, const_sem, out_sem, halo_send, halo_recv, late_recv, extra_send, extra_recv,
+    load_sem, const_sem, halo_send, halo_recv, late_recv, extra_send, extra_recv,
     send_x, sem_x, send_y, sem_y, send_z, sem_z,
 ):
     z = lax.axis_index("dp")
@@ -67,6 +70,7 @@
     right = {"dp": z, "ctx": lax.rem(c + 1, nc)}
     left = {"dp": z, "ctx": lax.rem(c + nc - 1, nc)}
     partner = {"dp": z, "ctx": c + 1 - 2 * core}
+    far = {"dp": z, "ctx": lax.rem(c + 2 * core - 1 + nc, nc)}
 
     def at(y_to, x_to, core_to):
         return {"dp": z, "ctx": y_to * (2 * NX) + x_to * 2 + core_to}
@@ -150,8 +154,9 @@
         )
 
     for j in range(nb):
-        halo_copy(0, near * nb + j, right).start()
-        halo_copy(1, near * nb + j, left).start()
+        halo_copy(near, near * nb + j, far).start()
+    for j in range(nb):
+        halo_copy(core, near * nb + j, partner).start()
         extra_copy(j).start()
 
     for copy in load(core):
@@ -173,6 +178,13 @@
             b = s * nb + j
             spec[0, b] = forward(own_ref[...], kg[0, b])
             spec[1, b] = forward(own_ref[...], kg[1, b])
+            return carry
+
+        lax.fori_loop(0, nb, step, 0)
+
+    def tap_spectra(s):
+        def step(j, carry):
+            b = s * nb + j
             taps = h_ref[:, pl.ds(pl.multiple_of(b * W, W), W)]
             spec_h[b] = forward(own_ref[...], taps)
             return carry
@@ -180,7 +192,6 @@
         lax.fori_loop(0, nb, step, 0)
 
     own_spectra(core)
-    own_spectra(near)
 
     def times(a, b):
         ar, ai, br, bi = a[:F], a[F:], b[:F], b[F:]
@@ -228,7 +239,7 @@
         re, im = times_conj(jnp.where(first, mate, slow), jnp.where(first, slow, mate))
         value = inverse(early_sum[j, :F] + re, early_sum[j, F:] + im)
         part_x[j] = jnp.transpose(value).astype(bf16).reshape(NX, W // NX, T)
-        for d in range(1, NX):
+        for d in (2, 1, 3):
             pltpu.make_async_remote_copy(
                 src_ref=part_x.at[j, lax.rem(x + d, NX)], dst_ref=recv_x.at[d - 1, j],
                 send_sem=send_x, recv_sem=sem_x, device_id=at_x(d), device_id_type=MESH,
@@ -236,8 +247,6 @@
         return carry
 
     lax.fori_loop(0, nb, gradient, 0)
-    late_copy(0, core, right).start()
-    late_copy(1, core, left).start()
 
     def outputs(s):
         def step(j, carry):
@@ -249,34 +258,26 @@
                 g_all += forward(prev_kg[1], halo[1, b])
             taps = spec_h[b]
             cols = pl.ds(pl.multiple_of(j * W, W), W)
+            full = pl.ds(pl.multiple_of(b * W, W), W)
             m = inverse(*times(k_all, taps))
-            q_ref[s, :, cols] = (q_ref[s, :, cols].astype(f32) * m).astype(bf16)
-            g_ref[s, :, cols] = (g_ref[s, :, cols].astype(f32) * m).astype(bf16)
+            y_hbm[0, :, full] = (q_ref[s, :, cols].astype(f32) * m).astype(bf16)
+            gq_hbm[0, :, full] = (g_ref[s, :, cols].astype(f32) * m).astype(bf16)
             m = inverse(*times_conj(g_all, taps))
-            v_ref[s, :, cols] = (v_ref[s, :, cols].astype(f32) * m).astype(bf16)
-            k_ref[s, :, cols] = (k_ref[s, :, cols].astype(f32) * m).astype(bf16)
+            gk_hbm[0, :, full] = (v_ref[s, :, cols].astype(f32) * m).astype(bf16)
+            gv_hbm[0, :, full] = (k_ref[s, :, cols].astype(f32) * m).astype(bf16)
             return carry
 
         lax.fori_loop(0, nb, step, 0)
-
-    def store(s):
-        cols = pl.ds(pl.multiple_of(s * half, half), half)
-        return [
-            pltpu.make_async_copy(src.at[s], dst.at[0, :, cols], out_sem.at[s, i])
-            for i, (src, dst) in enumerate(
-                [(q_ref, y_hbm), (g_ref, gq_hbm), (v_ref, gk_hbm), (k_ref, gv_hbm)]
-            )
-        ]
 
     def landed(ref, sem):
         pltpu.make_async_copy(ref, ref, sem).wait()
 
+    tap_spectra(core)
     outputs(core)
-    for copy in store(core):
-        copy.start()
 
     landed(recv_x, sem_x)
-    for j in range(nb):
+    for i in range(nb):
+        j = lax.rem(yy + i + jnp.where(own_source, 1, 0), nb)
         total = part_x[j, x].astype(f32)
         for d in range(NX - 1):
             total += recv_x[d, j].astype(f32)
@@ -295,6 +296,11 @@
             @pl.when(mine)
             def _():
                 recv_y[yy] = part_y[j, core_to]
+
+    late_copy(0, core, right).start()
+    late_copy(1, core, left).start()
+    own_spectra(near)
+    tap_spectra(near)
 
     for ys in range(ny):
         @pl.when(jnp.logical_not(jnp.logical_and(ys == yy, own_source)))
@@ -304,7 +310,7 @@
     for ys in range(1, ny):
         total += recv_y[ys].astype(f32)
     part_z[...] = total.astype(bf16)
-    for d in range(1, nz):
+    for d in sorted(range(1, nz), key=lambda d: abs(d - nz // 2)):
         pltpu.make_async_remote_copy(
             src_ref=part_z, dst_ref=recv_z.at[d - 1], send_sem=send_z, recv_sem=sem_z,
             device_id=at_z(d), device_id_type=MESH,
@@ -313,8 +319,6 @@
     late_copy(0, near, right).wait_recv()
     late_copy(1, near, left).wait_recv()
     outputs(near)
-    for copy in store(near):
-        copy.start()
 
     landed(recv_z, sem_z)
     total = part_z[...].astype(f32)
@@ -334,29 +338,14 @@
 
     landed(recv_z, send_z)
 
-    for s in (core, near):
-        for copy in store(s):
-            copy.wait()
-
 
 def write_out(*refs):
-    sources, targets, held, (load_sem, store_sem) = refs[:5], refs[5:10], refs[10:15], refs[15:]
-    rows = T // PIECES
-    loads, stores = [], []
-    for i in range(5):
-        for piece in range(PIECES if i < 4 else 1):
-            at = (0, pl.ds(piece * rows, rows)) if i < 4 else ()
-            loads.append(pltpu.make_async_copy(
-                sources[i].at[at], held[i].at[at], load_sem.at[i, piece]))
-            stores.append(pltpu.make_async_copy(
-                held[i].at[at], targets[i].at[at], store_sem.at[i, piece]))
-    for load in loads:
-        load.start()
-    for load, store in zip(loads, stores):
-        load.wait()
-        store.start()
-    for store in stores:
-        store.wait()
+    sem = refs[10]
+    copies = [pltpu.make_async_copy(refs[i], refs[5 + i], sem.at[i]) for i in range(5)]
+    for copy in copies:
+        copy.start()
+    for copy in copies:
+        copy.wait()
 
 
 def per_device(query_act, key_act, value_act, grad_out, filter_taps):
@@ -374,9 +363,9 @@
     limit = VMEM_BYTES
     outs = pl.pallas_call(
         functools.partial(kernel, nz, ny),
-        out_shape=[big] * 4 + [small],
+        out_shape=[pltpu.VMEM(big.shape, bf16)] * 4 + [pltpu.VMEM(small.shape, f32)],
         in_specs=[hbm] * 8,
-        out_specs=[hbm] * 4 + [vmem],
+        out_specs=[vmem] * 5,
         scratch_shapes=[
             *[pltpu.VMEM((2, T, half), bf16)] * 4,
             pltpu.VMEM((T, channels), bf16),
@@ -397,7 +386,7 @@
             pltpu.VMEM((ny, cols, T), bf16),
             pltpu.VMEM((cols, T), bf16),
             pltpu.VMEM((nz - 1, cols, T), bf16),
-            dma((2, 4)), dma((4,)), dma((2, 4)), dma((2,)), dma((2, ny // 2)), dma((2,)),
+            dma((2, 4)), dma((4,)), dma((2,)), dma((2, ny // 2)), dma((2,)),
             dma(()), dma((ny // 2,)), dma(()), dma(()), dma(()), dma((ny,)), dma(()), dma(()),
         ],
         compiler_params=pltpu.CompilerParams(
@@ -407,10 +396,10 @@
     *done, summed = pl.pallas_call(
         write_out,
         out_shape=[big] * 4 + [small],
-        in_specs=[hbm] * 5,
+        in_specs=[vmem] * 5,
         out_specs=[hbm] * 5,
-        scratch_shapes=[pltpu.VMEM(big.shape, bf16)] * 4 + [pltpu.VMEM(small.shape, f32)] + [dma((5, PIECES))] * 2,
-        compiler_params=pltpu.CompilerParams(vmem_limit_bytes=limit),
+        scratch_shapes=[dma((5,))],
+        compiler_params=pltpu.CompilerParams(vmem_limit_bytes=2**20),
     )(*outs)
     return (*done, summed.T)
 

time: 40.2 us -> 35.6 us (0.89)
  Pallas kernels: 39.4 us -> 34.8 us
    pallas_call x2, Pallas kernels: 39.4 us -> 34.8 us  [the longest x1 33.4 us: per_device(): pl.pallas_call(functools.partial(kernel, nz, ny), out_shape=[pltpu.VMEM(b...]
where the time goes in v3:
time: 35.6 us; the launch traced here: 35.4 us
  Pallas kernels  34.8 us (98%)
  between operations  0.64 us (2%)
    pallas_call x1, Pallas kernels, per_device(): pl.pallas_call(functools.partial(kernel, nz, ny), out_shape=[pltpu.VMEM(b...  33.4 us
    pallas_call x1, Pallas kernels, per_device(): pl.pallas_call(write_out, out_shape=[big] * 4 + [small], in_specs=[vmem]...  1.36 us

profile of v3, /device:TPU:1, one launch (start us, length us, event | category | flops | bytes accessed | tf_op | source)
XLA Modules:
  0.0 35.4 jit_solution(11171452570942442838)
XLA Ops:
  0.6 33.4 %shard_map.119 = (bf16[1,128,2048]{2,1,0:T(8,128)(2,1)S(1)}, bf16[1,128,2048]{2,1,0:T(8,128)(2,1)S(1)}, bf16[1,128,2048]{2,1,0:T(8,128)(2,1)S(1)}, bf16[1,128,2048]{2,1,0:T(8,128)(2,1)S(1)}, f32[32,128]{1,0:T(8,128)S(1)}) custom-call(bf16[1,128,2048]{2,1,0:T(8,128)(2,1)} %q_hbm.1, bf16[1,128,2048]{2,1,0:T(8,128)(2,1)} %k_hbm.1, bf16[1,128,2048]{2,1,0:T(8,128)(2,1)} %v_hbm.1, ...), custom_call_target="tpu_custom_call" | custom-call | tf_op jit(solution)/shard_map/pallas_call | solution.py:364
  34.1 1.4 %shard_map.120 = (bf16[1,128,2048]{2,1,0:T(8,128)(2,1)}, bf16[1,128,2048]{2,1,0:T(8,128)(2,1)}, bf16[1,128,2048]{2,1,0:T(8,128)(2,1)}, bf16[1,128,2048]{2,1,0:T(8,128)(2,1)}, f32[32,128]{1,0:T(8,128)}) custom-call(bf16[1,128,2048]{2,1,0:T(8,128)(2,1)S(1)} %get-tuple-element.15.refs_0_, bf16[1,128,2048]{2,1,0:T(8,128)(2,1)S(1)} %get-tuple-element.16.refs_1_, ...), custom_call_target="tpu_custom_call" | custom-call | tf_op jit(solution)/shard_map/pallas_call | solution.py:396

commit v4 on v3

--- a/solution.py
+++ b/solution.py
@@ -103,18 +103,22 @@
     def greet(device):
         pl.semaphore_signal(barrier, inc=1, device_id=device, device_id_type=MESH)
 
+    source_core = yy // nb
+    own_source = source_core == core
     greet(left)
     greet(right)
-    for d in range(1, NX):
+    for d in sorted(range(ny), key=lambda d: abs(d - ny // 2)):
+        ys = lax.rem(yy + d, ny)
+        if d:
+            greet(at(ys, x, source_core))
+        else:
+            @pl.when(jnp.logical_not(own_source))
+            def _():
+                greet(at(ys, x, source_core))
+    for d in (2, 1, 3):
         greet(at_x(d))
-    for d in range(1, nz):
+    for d in sorted(range(1, nz), key=lambda d: abs(d - nz // 2)):
         greet(at_z(d))
-    source_core = yy // nb
-    own_source = source_core == core
-    for ys in range(ny):
-        @pl.when(jnp.logical_not(jnp.logical_and(ys == yy, own_source)))
-        def _():
-            greet(at(ys, x, source_core))
 
     def products(s):
         for j in range(nb):
@@ -139,12 +143,22 @@
             device_id=device, device_id_type=MESH,
         )
 
-    def late_copy(array, s, device):
+    def late_copy(array, b, device):
         return pltpu.make_async_remote_copy(
-            src_ref=kg.at[array, pl.ds(s * nb, nb)], dst_ref=halo.at[array, pl.ds(s * nb, nb)],
-            send_sem=halo_send.at[array], recv_sem=late_recv.at[array],
+            src_ref=kg.at[array, b], dst_ref=halo.at[array, b],
+            send_sem=halo_send.at[array], recv_sem=late_recv.at[array, b % nb],
             device_id=device, device_id_type=MESH,
         )
+
+    def send_late(first_block, last_block):
+        for j in range(first_block, last_block):
+            late_copy(near, core * nb + j, far).start()
+
+    def send_near():
+        for j in range(nb):
+            late_copy(core, core * nb + j, partner).start()
+
+    turn = x == jnp.where(core == 1, NX - 1, 0)
 
     def extra_copy(j):
         return pltpu.make_async_remote_copy(
@@ -241,16 +255,23 @@
         part_x[j] = jnp.transpose(value).astype(bf16).reshape(NX, W // NX, T)
         for d in (2, 1, 3):
             pltpu.make_async_remote_copy(
-                src_ref=part_x.at[j, lax.rem(x + d, NX)], dst_ref=recv_x.at[d - 1, j],
-                send_sem=send_x, recv_sem=sem_x, device_id=at_x(d), device_id_type=MESH,
+                src_ref=part_x.at[j, lax.rem(x + d, NX)], dst_ref=recv_x.at[j, d - 1],
+                send_sem=send_x, recv_sem=sem_x.at[j], device_id=at_x(d), device_id_type=MESH,
             ).start()
         return carry
 
     lax.fori_loop(0, nb, gradient, 0)
-
-    def outputs(s):
+    @pl.when(turn)
+    def _():
+        send_late(0, nb // 2)
+
+
+    def outputs(s, first_block, last_block):
         def step(j, carry):
             b = s * nb + j
+            if s is near:
+                late_copy(0, b, right).wait_recv()
+                late_copy(1, b, left).wait_recv()
             k_all = spec[0, b]
             g_all = spec[1, b]
             if s is near:
@@ -267,20 +288,18 @@
             gv_hbm[0, :, full] = (k_ref[s, :, cols].astype(f32) * m).astype(bf16)
             return carry
 
-        lax.fori_loop(0, nb, step, 0)
+        lax.fori_loop(first_block, last_block, step, 0)
 
     def landed(ref, sem):
         pltpu.make_async_copy(ref, ref, sem).wait()
 
-    tap_spectra(core)
-    outputs(core)
-
-    landed(recv_x, sem_x)
-    for i in range(nb):
-        j = lax.rem(yy + i + jnp.where(own_source, 1, 0), nb)
+    own_spectra(near)
+
+    for j in range(nb):
+        landed(recv_x.at[j], sem_x.at[j])
         total = part_x[j, x].astype(f32)
         for d in range(NX - 1):
-            total += recv_x[d, j].astype(f32)
+            total += recv_x[j, d].astype(f32)
         part_y[j] = total.astype(bf16).reshape(2, W // NX // 2, T)
         for core_to in range(2):
             mine = jnp.logical_and(jnp.logical_and(own_source, yy == core * nb + j), core == core_to)
@@ -297,10 +316,14 @@
             def _():
                 recv_y[yy] = part_y[j, core_to]
 
-    late_copy(0, core, right).start()
-    late_copy(1, core, left).start()
-    own_spectra(near)
+    send_near()
+    @pl.when(jnp.logical_not(turn))
+    def _():
+        send_late(0, nb)
+
+    tap_spectra(core)
     tap_spectra(near)
+    outputs(core, 0, nb)
 
     for ys in range(ny):
         @pl.when(jnp.logical_not(jnp.logical_and(ys == yy, own_source)))
@@ -316,9 +339,11 @@
             device_id=at_z(d), device_id_type=MESH,
         ).start()
 
-    late_copy(0, near, right).wait_recv()
-    late_copy(1, near, left).wait_recv()
-    outputs(near)
+    @pl.when(turn)
+    def _():
+        send_late(nb // 2, nb)
+
+    outputs(near, 0, nb)
 
     landed(recv_z, sem_z)
     total = part_z[...].astype(f32)
@@ -381,13 +406,13 @@
             pltpu.VMEM((ny // 2, 2 * F, W), f32),
             pltpu.VMEM((ny // 2, 2 * F, W), f32),
             pltpu.VMEM((ny // 2, NX, W // NX, T), bf16),
-            pltpu.VMEM((NX - 1, ny // 2, W // NX, T), bf16),
+            pltpu.VMEM((ny // 2, NX - 1, W // NX, T), bf16),
             pltpu.VMEM((ny // 2, 2, cols, T), bf16),
             pltpu.VMEM((ny, cols, T), bf16),
             pltpu.VMEM((cols, T), bf16),
             pltpu.VMEM((nz - 1, cols, T), bf16),
-            dma((2, 4)), dma((4,)), dma((2,)), dma((2, ny // 2)), dma((2,)),
-            dma(()), dma((ny // 2,)), dma(()), dma(()), dma(()), dma((ny,)), dma(()), dma(()),
+            dma((2, 4)), dma((4,)), dma((2,)), dma((2, ny // 2)), dma((2, ny // 2)),
+            dma(()), dma((ny // 2,)), dma(()), dma((ny // 2,)), dma(()), dma((ny,)), dma(()), dma(()),
         ],
         compiler_params=pltpu.CompilerParams(
             collective_id=1, has_side_effects=True, vmem_limit_bytes=limit

time: 35.6 us -> 34.3 us (0.963)
  Pallas kernels: 34.8 us -> 33.5 us
    pallas_call x1, Pallas kernels: 33.4 us -> 32.1 us  [per_device(): pl.pallas_call(functools.partial(kernel, nz, ny), out_shape=[pltpu.VMEM(b...]
where the time goes in v4:
time: 34.3 us; the launch traced here: 34.1 us
  Pallas kernels  33.5 us (98%)
  between operations  0.64 us (2%)
    pallas_call x1, Pallas kernels, per_device(): pl.pallas_call(functools.partial(kernel, nz, ny), out_shape=[pltpu.VMEM(b...  32.1 us
    pallas_call x1, Pallas kernels, per_device(): pl.pallas_call(write_out, out_shape=[big] * 4 + [small], in_specs=[vmem]...  1.36 us

profile of v4, /device:TPU:1, one launch (start us, length us, event | category | flops | bytes accessed | tf_op | source)
XLA Modules:
  0.0 34.1 jit_solution(5102786415807878432)
XLA Ops:
  0.6 32.1 %shard_map.119 = (bf16[1,128,2048]{2,1,0:T(8,128)(2,1)S(1)}, bf16[1,128,2048]{2,1,0:T(8,128)(2,1)S(1)}, bf16[1,128,2048]{2,1,0:T(8,128)(2,1)S(1)}, bf16[1,128,2048]{2,1,0:T(8,128)(2,1)S(1)}, f32[32,128]{1,0:T(8,128)S(1)}) custom-call(bf16[1,128,2048]{2,1,0:T(8,128)(2,1)} %q_hbm.1, bf16[1,128,2048]{2,1,0:T(8,128)(2,1)} %k_hbm.1, bf16[1,128,2048]{2,1,0:T(8,128)(2,1)} %v_hbm.1, ...), custom_call_target="tpu_custom_call" | custom-call | tf_op jit(solution)/shard_map/pallas_call | solution.py:389
  32.7 1.4 %shard_map.120 = (bf16[1,128,2048]{2,1,0:T(8,128)(2,1)}, bf16[1,128,2048]{2,1,0:T(8,128)(2,1)}, bf16[1,128,2048]{2,1,0:T(8,128)(2,1)}, bf16[1,128,2048]{2,1,0:T(8,128)(2,1)}, f32[32,128]{1,0:T(8,128)}) custom-call(bf16[1,128,2048]{2,1,0:T(8,128)(2,1)S(1)} %get-tuple-element.15.refs_0_, bf16[1,128,2048]{2,1,0:T(8,128)(2,1)S(1)} %get-tuple-element.16.refs_1_, ...), custom_call_target="tpu_custom_call" | custom-call | tf_op jit(solution)/shard_map/pallas_call | solution.py:421

commit v5 on v4

--- a/solution.py
+++ b/solution.py
@@ -105,6 +105,8 @@
 
     source_core = yy // nb
     own_source = source_core == core
+    for d in sorted(range(1, nz), key=lambda d: abs(d - nz // 2)):
+        greet(at_z(d))
     greet(left)
     greet(right)
     for d in sorted(range(ny), key=lambda d: abs(d - ny // 2)):
@@ -117,8 +119,6 @@
                 greet(at(ys, x, source_core))
     for d in (2, 1, 3):
         greet(at_x(d))
-    for d in sorted(range(1, nz), key=lambda d: abs(d - nz // 2)):
-        greet(at_z(d))
 
     def products(s):
         for j in range(nb):
@@ -325,6 +325,11 @@
     tap_spectra(near)
     outputs(core, 0, nb)
 
+    @pl.when(turn)
+    def _():
+        send_late(nb // 2, nb)
+
+
     for ys in range(ny):
         @pl.when(jnp.logical_not(jnp.logical_and(ys == yy, own_source)))
         def _():
@@ -339,27 +344,23 @@
             device_id=at_z(d), device_id_type=MESH,
         ).start()
 
-    @pl.when(turn)
+    outputs(near, 0, nb)
+
+    landed(kg.at[0], halo_send.at[0])
+    landed(kg.at[1], halo_send.at[1])
+    landed(extra, extra_send)
+    landed(recv_x, send_x)
+    landed(recv_y.at[pl.ds(0, ny - 1)], send_y)
+
+    @pl.when(jnp.logical_not(own_source))
     def _():
-        send_late(nb // 2, nb)
-
-    outputs(near, 0, nb)
+        landed(recv_y.at[ny - 1], send_y)
 
     landed(recv_z, sem_z)
     total = part_z[...].astype(f32)
     for d in range(nz - 1):
         total += recv_z[d].astype(f32)
     gf_ref[...] = total * (1.0 / math.sqrt(T * nc * nz))
-
-    landed(kg.at[0], halo_send.at[0])
-    landed(kg.at[1], halo_send.at[1])
-    landed(extra, extra_send)
-    landed(recv_x, send_x)
-    landed(recv_y.at[pl.ds(0, ny - 1)], send_y)
-
-    @pl.when(jnp.logical_not(own_source))
-    def _():
-        landed(recv_y.at[ny - 1], send_y)
 
     landed(recv_z, send_z)
 

time: 34.3 us -> 34.2 us (level)
  no operation moved by 1% of the time
where the time goes in v5:
time: 34.2 us; the launch traced here: 34.1 us
  Pallas kernels  33.5 us (98%)
  between operations  0.64 us (2%)
    pallas_call x1, Pallas kernels, per_device(): pl.pallas_call(functools.partial(kernel, nz, ny), out_shape=[pltpu.VMEM(b...  32.1 us
    pallas_call x1, Pallas kernels, per_device(): pl.pallas_call(write_out, out_shape=[big] * 4 + [small], in_specs=[vmem]...  1.36 us

profile of v5, /device:TPU:1, one launch (start us, length us, event | category | flops | bytes accessed | tf_op | source)
XLA Modules:
  0.0 34.1 jit_solution(10914408780964648382)
XLA Ops:
  0.6 32.1 %shard_map.119 = (bf16[1,128,2048]{2,1,0:T(8,128)(2,1)S(1)}, bf16[1,128,2048]{2,1,0:T(8,128)(2,1)S(1)}, bf16[1,128,2048]{2,1,0:T(8,128)(2,1)S(1)}, bf16[1,128,2048]{2,1,0:T(8,128)(2,1)S(1)}, f32[32,128]{1,0:T(8,128)S(1)}) custom-call(bf16[1,128,2048]{2,1,0:T(8,128)(2,1)} %q_hbm.1, bf16[1,128,2048]{2,1,0:T(8,128)(2,1)} %k_hbm.1, bf16[1,128,2048]{2,1,0:T(8,128)(2,1)} %v_hbm.1, ...), custom_call_target="tpu_custom_call" | custom-call | tf_op jit(solution)/shard_map/pallas_call | solution.py:390
  32.7 1.4 %shard_map.120 = (bf16[1,128,2048]{2,1,0:T(8,128)(2,1)}, bf16[1,128,2048]{2,1,0:T(8,128)(2,1)}, bf16[1,128,2048]{2,1,0:T(8,128)(2,1)}, bf16[1,128,2048]{2,1,0:T(8,128)(2,1)}, f32[32,128]{1,0:T(8,128)}) custom-call(bf16[1,128,2048]{2,1,0:T(8,128)(2,1)S(1)} %get-tuple-element.15.refs_0_, bf16[1,128,2048]{2,1,0:T(8,128)(2,1)S(1)} %get-tuple-element.16.refs_1_, ...), custom_call_target="tpu_custom_call" | custom-call | tf_op jit(solution)/shard_map/pallas_call | solution.py:422

commit v6 on v5

--- a/solution.py
+++ b/solution.py
@@ -143,6 +143,14 @@
             device_id=device, device_id_type=MESH,
         )
 
+    def half_copy(array, b, part, device):
+        lanes = pl.ds(part * (W // 2), W // 2)
+        return pltpu.make_async_remote_copy(
+            src_ref=kg.at[array, b, :, lanes], dst_ref=halo.at[array, b, :, lanes],
+            send_sem=halo_send.at[array], recv_sem=halo_recv.at[array, nb - 1 + part],
+            device_id=device, device_id_type=MESH,
+        )
+
     def late_copy(array, b, device):
         return pltpu.make_async_remote_copy(
             src_ref=kg.at[array, b], dst_ref=halo.at[array, b],
@@ -167,8 +175,10 @@
             device_id=partner, device_id_type=MESH,
         )
 
-    for j in range(nb):
+    for j in range(nb - 1):
         halo_copy(near, near * nb + j, far).start()
+    for part in range(2):
+        half_copy(near, near * nb + nb - 1, part, far).start()
     for j in range(nb):
         halo_copy(core, near * nb + j, partner).start()
         extra_copy(j).start()
@@ -243,24 +253,39 @@
 
     lax.fori_loop(0, nb, early_terms, 0)
 
+    def slow_terms(j, lanes):
+        b = core * nb + j
+        slow = forward(prev_kg[core], halo[core, b, :, lanes])
+        spec[core, b, :, lanes] = spec[core, b, :, lanes] + slow
+        mate = mates[j, :, lanes]
+        re, im = times_conj(jnp.where(first, mate, slow), jnp.where(first, slow, mate))
+        value = inverse(early_sum[j, :F, lanes] + re, early_sum[j, F:, lanes] + im)
+        return jnp.transpose(value).astype(bf16)
+
+    def send_block(j, d):
+        pltpu.make_async_remote_copy(
+            src_ref=part_x.at[j, lax.rem(x + d, NX)], dst_ref=recv_x.at[j, d - 1],
+            send_sem=send_x, recv_sem=sem_x.at[j], device_id=at_x(d), device_id_type=MESH,
+        ).start()
+
     def gradient(j, carry):
-        b = core * nb + j
-        halo_copy(core, b, partner).wait_recv()
-        slow = forward(prev_kg[core], halo[core, b])
-        own = spec[core, b]
-        spec[core, b] = own + slow
-        mate = mates[j]
-        re, im = times_conj(jnp.where(first, mate, slow), jnp.where(first, slow, mate))
-        value = inverse(early_sum[j, :F] + re, early_sum[j, F:] + im)
-        part_x[j] = jnp.transpose(value).astype(bf16).reshape(NX, W // NX, T)
+        halo_copy(core, core * nb + j, partner).wait_recv()
+        part_x[j] = slow_terms(j, slice(None)).reshape(NX, W // NX, T)
         for d in (2, 1, 3):
-            pltpu.make_async_remote_copy(
-                src_ref=part_x.at[j, lax.rem(x + d, NX)], dst_ref=recv_x.at[j, d - 1],
-                send_sem=send_x, recv_sem=sem_x.at[j], device_id=at_x(d), device_id_type=MESH,
-            ).start()
+            send_block(j, d)
         return carry
 
-    lax.fori_loop(0, nb, gradient, 0)
+    lax.fori_loop(0, nb - 1, gradient, 0)
+    for part in range(2):
+        half_copy(core, core * nb + nb - 1, part, partner).wait_recv()
+        lanes = slice(part * (W // 2), (part + 1) * (W // 2))
+        owners = slice(part * (NX // 2), (part + 1) * (NX // 2))
+        part_x[nb - 1, owners] = slow_terms(nb - 1, lanes).reshape(NX // 2, W // NX, T)
+        for d in (2, 1, 3):
+            @pl.when(lax.rem(x + d, NX) // (NX // 2) == part)
+            def _():
+                send_block(nb - 1, d)
+
     @pl.when(turn)
     def _():
         send_late(0, nb // 2)
@@ -412,7 +437,7 @@
             pltpu.VMEM((ny, cols, T), bf16),
             pltpu.VMEM((cols, T), bf16),
             pltpu.VMEM((nz - 1, cols, T), bf16),
-            dma((2, 4)), dma((4,)), dma((2,)), dma((2, ny // 2)), dma((2, ny // 2)),
+            dma((2, 4)), dma((4,)), dma((2,)), dma((2, ny // 2 + 1)), dma((2, ny // 2)),
             dma(()), dma((ny // 2,)), dma(()), dma((ny // 2,)), dma(()), dma((ny,)), dma(()), dma(()),
         ],
         compiler_params=pltpu.CompilerParams(

time: 34.2 us -> 34.3 us (level)
  no operation moved by 1% of the time
where the time goes in v6:
time: 34.3 us; the launch traced here: 34.1 us
  Pallas kernels  33.5 us (98%)
  between operations  0.64 us (2%)
    pallas_call x1, Pallas kernels, per_device(): pl.pallas_call(functools.partial(kernel, nz, ny), out_shape=[pltpu.VMEM(b...  32.1 us
    pallas_call x1, Pallas kernels, per_device(): pl.pallas_call(write_out, out_shape=[big] * 4 + [small], in_specs=[vmem]...  1.36 us

profile of v6, /device:TPU:1, one launch (start us, length us, event | category | flops | bytes accessed | tf_op | source)
XLA Modules:
  0.0 34.1 jit_solution(15183465040524016699)
XLA Ops:
  0.6 32.1 %shard_map.119 = (bf16[1,128,2048]{2,1,0:T(8,128)(2,1)S(1)}, bf16[1,128,2048]{2,1,0:T(8,128)(2,1)S(1)}, bf16[1,128,2048]{2,1,0:T(8,128)(2,1)S(1)}, bf16[1,128,2048]{2,1,0:T(8,128)(2,1)S(1)}, f32[32,128]{1,0:T(8,128)S(1)}) custom-call(bf16[1,128,2048]{2,1,0:T(8,128)(2,1)} %q_hbm.1, bf16[1,128,2048]{2,1,0:T(8,128)(2,1)} %k_hbm.1, bf16[1,128,2048]{2,1,0:T(8,128)(2,1)} %v_hbm.1, ...), custom_call_target="tpu_custom_call" | custom-call | tf_op jit(solution)/shard_map/pallas_call | solution.py:415
  32.8 1.4 %shard_map.120 = (bf16[1,128,2048]{2,1,0:T(8,128)(2,1)}, bf16[1,128,2048]{2,1,0:T(8,128)(2,1)}, bf16[1,128,2048]{2,1,0:T(8,128)(2,1)}, bf16[1,128,2048]{2,1,0:T(8,128)(2,1)}, f32[32,128]{1,0:T(8,128)}) custom-call(bf16[1,128,2048]{2,1,0:T(8,128)(2,1)S(1)} %get-tuple-element.15.refs_0_, bf16[1,128,2048]{2,1,0:T(8,128)(2,1)S(1)} %get-tuple-element.16.refs_1_, ...), custom_call_target="tpu_custom_call" | custom-call | tf_op jit(solution)/shard_map/pallas_call | solution.py:447

commit v7 on v5

--- a/solution.py
+++ b/solution.py
@@ -247,8 +247,6 @@
         b = core * nb + j
         halo_copy(core, b, partner).wait_recv()
         slow = forward(prev_kg[core], halo[core, b])
-        own = spec[core, b]
-        spec[core, b] = own + slow
         mate = mates[j]
         re, im = times_conj(jnp.where(first, mate, slow), jnp.where(first, slow, mate))
         value = inverse(early_sum[j, :F] + re, early_sum[j, F:] + im)
@@ -258,9 +256,10 @@
                 src_ref=part_x.at[j, lax.rem(x + d, NX)], dst_ref=recv_x.at[j, d - 1],
                 send_sem=send_x, recv_sem=sem_x.at[j], device_id=at_x(d), device_id_type=MESH,
             ).start()
+        spec[core, b] = spec[core, b] + slow
         return carry
 
-    lax.fori_loop(0, nb, gradient, 0)
+    lax.fori_loop(0, nb, gradient, 0, unroll=True)
     @pl.when(turn)
     def _():
         send_late(0, nb // 2)

time: 34.2 us -> 34.2 us (level)
  no operation moved by 1% of the time
where the time goes in v7:
time: 34.2 us; the launch traced here: 34.1 us
  Pallas kernels  33.4 us (98%)
  between operations  0.64 us (2%)
    pallas_call x1, Pallas kernels, per_device(): pl.pallas_call(functools.partial(kernel, nz, ny), out_shape=[pltpu.VMEM(b...  32.1 us
    pallas_call x1, Pallas kernels, per_device(): pl.pallas_call(write_out, out_shape=[big] * 4 + [small], in_specs=[vmem]...  1.36 us

profile of v7, /device:TPU:1, one launch (start us, length us, event | category | flops | bytes accessed | tf_op | source)
XLA Modules:
  0.0 34.1 jit_solution(9948792092680570458)
XLA Ops:
  0.6 32.1 %shard_map.119 = (bf16[1,128,2048]{2,1,0:T(8,128)(2,1)S(1)}, bf16[1,128,2048]{2,1,0:T(8,128)(2,1)S(1)}, bf16[1,128,2048]{2,1,0:T(8,128)(2,1)S(1)}, bf16[1,128,2048]{2,1,0:T(8,128)(2,1)S(1)}, f32[32,128]{1,0:T(8,128)S(1)}) custom-call(bf16[1,128,2048]{2,1,0:T(8,128)(2,1)} %q_hbm.1, bf16[1,128,2048]{2,1,0:T(8,128)(2,1)} %k_hbm.1, bf16[1,128,2048]{2,1,0:T(8,128)(2,1)} %v_hbm.1, ...), custom_call_target="tpu_custom_call" | custom-call | tf_op jit(solution)/shard_map/pallas_call | solution.py:389
  32.7 1.4 %shard_map.120 = (bf16[1,128,2048]{2,1,0:T(8,128)(2,1)}, bf16[1,128,2048]{2,1,0:T(8,128)(2,1)}, bf16[1,128,2048]{2,1,0:T(8,128)(2,1)}, bf16[1,128,2048]{2,1,0:T(8,128)(2,1)}, f32[32,128]{1,0:T(8,128)}) custom-call(bf16[1,128,2048]{2,1,0:T(8,128)(2,1)S(1)} %get-tuple-element.15.refs_0_, bf16[1,128,2048]{2,1,0:T(8,128)(2,1)S(1)} %get-tuple-element.16.refs_1_, ...), custom_call_target="tpu_custom_call" | custom-call | tf_op jit(solution)/shard_map/pallas_call | solution.py:421
